TPU v7x, 32 devices: a whole 2x2x4 slice. The times are simulated.
32 devices in a mesh: group: 2 (over y), expert: 4 (over z), dp: 2 (over x), tensor: 2 (over core).
Axes of the slice: x: 2, y: 2, z: 4, core: 2. Of those that a mesh axis runs over, the one named last changes fastest.
Arguments:
- incoming_activation_vectors: bfloat16 [1024, 3072], P(('group', 'expert', 'dp'), 'tensor'), parts along dimension 0, may hold values from -6 to 6
- routed_specialist_pairs: int32 [1024, 2], P(('group', 'expert', 'dp')), parts along dimension 0, may hold values from 0 to 3, as said below
- routing_shares: float32 [1024, 2], P(('group', 'expert', 'dp')), parts along dimension 0, may hold values from 0.2 to 1
- popular_specialist_flags: int32 [8], P('group'), parts along dimension 0, may hold values from 0 to 1, as said below
- group_quotas: int32 [8], P('group'), parts along dimension 0, may hold values from 8 to 16
- gating_weight_stack: bfloat16 [3072, 32768], P('dp', ('expert', 'tensor')), may hold values from -0.109375 to 0.109375
- widen_weight_stack: bfloat16 [3072, 32768], P('dp', ('expert', 'tensor')), may hold values from -0.109375 to 0.109375
- contract_weight_stack: bfloat16 [32768, 3072], P(('expert', 'tensor'), 'dp'), may hold values from -0.0625 to 0.0625
Outputs:
- mixed: bfloat16 [1024, 3072], P(('group', 'expert', 'dp'), 'tensor'), parts along dimension 0
There are 2 independent parts, one for each index of `group`. A program takes and returns all parts, laid end to end along the dimension named above; an argument that names none is the same for every part. Nothing has to cross between parts.
Inputs may be any that keep to these rules, and one draw needn't show every extreme that they name: `routed_specialist_pairs`: each token names two different experts. Every expert with popular_specialist_flags 1 is named by at least 32 tokens of every aligned block of 64 tokens. `popular_specialist_flags`: one or two experts have the value 1.
All inputs are finite; a program needn't handle non-finite values.
Results may differ from a plain program's by a relative error of at most 0.0058.
Values may be sent and summed in bfloat16 or wider, within the bound.
A program may use at most 256 MiB of HBM per device.

v0:
```python
import jax
import jax.numpy as jnp
from jax import lax
from jax.experimental import pallas as pl
from jax.experimental.pallas import tpu as pltpu
from jax.sharding import PartitionSpec as P

GROUP_QUOTA = 32
EXPERTS = 4


def gathered(
    incoming_activation_vectors,
    routed_specialist_pairs,
    routing_shares,
    popular_specialist_flags,
    group_quotas,
    gating_weight_stack,
    widen_weight_stack,
    contract_weight_stack,
):
    experts = popular_specialist_flags.shape[0]
    tok_rows = incoming_activation_vectors.shape[0]
    half_width = incoming_activation_vectors.shape[1]
    expert_count = lax.axis_size("expert")
    tensor_count = lax.axis_size("tensor")
    owners = expert_count // experts
    pair_ids = routed_specialist_pairs.reshape(-1)
    onehot = (pair_ids[:, None] == jnp.arange(experts, dtype=jnp.int32)[None, :]).astype(jnp.int32)
    slot_rank = jnp.sum((jnp.cumsum(onehot, axis=0) - onehot) * onehot, axis=1)
    quota_bound = jnp.where(popular_specialist_flags == 1, GROUP_QUOTA, group_quotas)
    kept_pair = slot_rank < jnp.sum(onehot * quota_bound[None, :], axis=1)
    target = jnp.where(kept_pair, pair_ids * GROUP_QUOTA + slot_rank, -1)
    select = (
        jnp.arange(experts * GROUP_QUOTA, dtype=jnp.int32)[:, None] == target[None, :]
    ).astype(jnp.bfloat16)
    select = select.reshape(experts * GROUP_QUOTA, tok_rows, 2).sum(axis=2)
    packed = jnp.dot(
        select, incoming_activation_vectors, preferred_element_type=jnp.float32
    ).astype(jnp.bfloat16)
    packed = packed.reshape(experts, GROUP_QUOTA, half_width)
    outgoing = jnp.repeat(packed, owners * tensor_count, axis=0)
    arrived = lax.all_to_all(
        outgoing, ("expert", "tensor"), split_axis=0, concat_axis=2, tiled=True
    )
    owner_rows = arrived.reshape(GROUP_QUOTA * expert_count, half_width * tensor_count)
    gate_part = jnp.dot(
        owner_rows,
        lax.all_gather(gating_weight_stack, "dp", axis=0, tiled=True),
        preferred_element_type=jnp.float32,
    )
    up_part = jnp.dot(
        owner_rows,
        lax.all_gather(widen_weight_stack, "dp", axis=0, tiled=True),
        preferred_element_type=jnp.float32,
    )
    hidden = (jax.nn.silu(gate_part) * up_part).astype(jnp.bfloat16)
    partial_value = jnp.dot(
        hidden,
        lax.all_gather(contract_weight_stack, "dp", axis=1, tiled=True),
        preferred_element_type=jnp.float32,
    )
    partial_value = partial_value.astype(jnp.bfloat16).reshape(
        1, GROUP_QUOTA, expert_count * tensor_count * half_width
    )
    returned = lax.all_to_all(
        partial_value, ("expert", "tensor"), split_axis=2, concat_axis=0, tiled=True
    )
    summed = (
        returned.astype(jnp.float32)
        .reshape(experts, owners * tensor_count, GROUP_QUOTA, half_width)
        .sum(axis=1)
    )
    summed = summed.reshape(experts * GROUP_QUOTA, half_width)
    pick_index = jnp.maximum(target, 0)
    weights_kept = jnp.where(kept_pair, routing_shares.reshape(-1), 0.0)
    picked = jnp.take(summed, pick_index, axis=0) * weights_kept[:, None]
    mixed = picked.reshape(tok_rows, 2, half_width).sum(axis=1)
    return mixed.astype(jnp.bfloat16)


def route(routed_specialist_pairs, popular_specialist_flags, group_quotas):
    experts = popular_specialist_flags.shape[0]
    pair_ids = routed_specialist_pairs.reshape(-1)
    onehot = (pair_ids[:, None] == jnp.arange(experts, dtype=jnp.int32)[None, :]).astype(jnp.int32)
    slot_rank = jnp.sum((jnp.cumsum(onehot, axis=0) - onehot) * onehot, axis=1)
    quota_bound = jnp.where(popular_specialist_flags == 1, GROUP_QUOTA, group_quotas)
    kept_pair = slot_rank < jnp.sum(onehot * quota_bound[None, :], axis=1)
    return kept_pair, jnp.where(kept_pair, pair_ids * GROUP_QUOTA + slot_rank, -1)


HOPS = 4
PARTS = 4
STEPS = HOPS * PARTS
LAG_SUM = 3
LAG_DOWN = 3


def flip(e, k):
    low = lax.rem(lax.rem(e, 2) + lax.rem(k, 2), 2)
    high = lax.rem(lax.div(e, 2) + lax.div(k, 2), 2)
    return low + 2 * high


def layer_kernel(
    packed,
    gate_hbm,
    up_hbm,
    down_hbm,
    out,
    gate_w,
    up_w,
    down_w,
    rows,
    keep,
    part_out,
    part_in,
    hid,
    acc,
    core_in,
    back,
    w_sem,
    disp_send,
    disp_recv,
    fwd_send,
    fwd_recv,
    self_sem,
    part_send,
    part_recv,
    hid_send,
    hid_recv,
    core_send,
    core_recv,
    back_send,
    back_recv,
):
    e = lax.axis_index("expert")
    d = lax.axis_index("dp")
    t = lax.axis_index("tensor")
    quota = packed.shape[1]
    width = gate_w.shape[2]
    mesh_ids = pl.DeviceIdType.MESH
    home = d == t
    direct = lax.rem(d + t, 2)

    def weight_copy(which, j):
        hbm, vmem = ((gate_hbm, gate_w), (up_hbm, up_w), (down_hbm, down_w))[which]
        start = pl.multiple_of(j * width, width)
        block = hbm.at[pl.ds(start, width), :] if which == 2 else hbm.at[:, pl.ds(start, width)]
        return pltpu.make_async_copy(block, vmem.at[j], w_sem.at[which, j])

    def far(k):
        return {"expert": flip(e, k), "dp": t, "tensor": d}

    sibling = {"expert": e, "dp": d, "tensor": 1 - t}
    across = {"expert": e, "dp": 1 - d, "tensor": t}

    def remote(src, dst, send, recv, target):
        return pltpu.make_async_remote_copy(
            src_ref=src,
            dst_ref=dst,
            send_sem=send,
            recv_sem=recv,
            device_id=target,
            device_id_type=mesh_ids,
        )

    def dispatch(k):
        return remote(
            packed.at[k], rows.at[k, direct], disp_send.at[k], disp_recv.at[k], far(k)
        )

    def dispatch_self():
        return pltpu.make_async_copy(packed.at[0], rows.at[0, direct], self_sem)

    def forward(k):
        return remote(
            rows.at[k, direct], rows.at[k, direct], fwd_send.at[k], fwd_recv.at[k], sibling
        )

    def part_copy(s):
        return remote(part_out.at[s], part_in.at[s], part_send.at[s], part_recv.at[s], across)

    def hid_copy(s):
        return remote(hid.at[s, 0], hid.at[s, 1], hid_send.at[s], hid_recv.at[s], across)

    def core_copy(k):
        return remote(acc.at[k, 1 - direct], core_in.at[k], core_send.at[k], core_recv.at[k], sibling)

    def back_copy(k):
        return remote(back.at[k], out.at[k], back_send.at[k], back_recv.at[k], far(k))

    for j in range(PARTS):
        weight_copy(0, j).start()
        weight_copy(1, j).start()
    for j in range(PARTS):
        weight_copy(2, j).start()

    barrier = pltpu.get_barrier_semaphore()
    for target in (sibling, across, far(1), far(2), far(3)):
        pl.semaphore_signal(barrier, inc=1, device_id=target, device_id_type=mesh_ids)

    @pl.when(home)
    def _():
        pl.semaphore_wait(barrier, 5)
        dispatch_self().start()

    @pl.when(jnp.logical_not(home))
    def _():
        pl.semaphore_signal(barrier, inc=1, device_id=far(0), device_id_type=mesh_ids)
        pl.semaphore_wait(barrier, 6)
        dispatch(0).start()

    for k in range(1, HOPS):
        dispatch(k).start()

    @pl.when(home)
    def _():
        dispatch_self().wait()

    @pl.when(jnp.logical_not(home))
    def _():
        dispatch(0).wait_recv()

    forward(0).start()
    forward(0).wait_recv()

    def body(s, carry):
        k = lax.div(s, PARTS)
        j = lax.rem(s, PARTS)

        @pl.when(s < STEPS)
        def _():
            @pl.when(jnp.logical_and(j == 0, k > 0))
            def _():
                forward(k).wait_recv()

            @pl.when(k == 0)
            def _():
                weight_copy(0, j).wait()
                weight_copy(1, j).wait()

            block = rows[k].reshape(2 * quota, rows.shape[3])
            gate = jnp.dot(block, gate_w[j], preferred_element_type=jnp.float32)
            keep[s, 0] = gate[:quota]
            part_out[s, 0] = gate[quota:].astype(jnp.bfloat16)
            up = jnp.dot(block, up_w[j], preferred_element_type=jnp.float32)
            keep[s, 1] = up[:quota]
            part_out[s, 1] = up[quota:].astype(jnp.bfloat16)
            part_copy(s).start()

            @pl.when(jnp.logical_and(j == PARTS // 2, k < HOPS - 1))
            def _():
                dispatch(k + 1).wait_recv()
                forward(k + 1).start()

        h = s - LAG_SUM

        @pl.when(jnp.logical_and(h >= 0, h < STEPS))
        def _():
            part_copy(h).wait_recv()
            gate = keep[h, 0] + part_in[h, 0].astype(jnp.float32)
            up = keep[h, 1] + part_in[h, 1].astype(jnp.float32)
            hid[h, 0] = (gate / (1.0 + jnp.exp(-gate)) * up).astype(jnp.bfloat16)
            hid_copy(h).start()

        q = s - LAG_SUM - LAG_DOWN

        @pl.when(q >= 0)
        def _():
            kq = lax.div(q, PARTS)
            jq = lax.rem(q, PARTS)
            hid_copy(q).wait_recv()

            @pl.when(kq == 0)
            def _():
                weight_copy(2, jq).wait()

            term = jnp.dot(
                hid[q].reshape(2 * quota, width), down_w[jq], preferred_element_type=jnp.float32
            ).reshape(2, quota, acc.shape[3])

            @pl.when(jq == 0)
            def _():
                acc[kq] = term

            @pl.when(jq > 0)
            def _():
                acc[kq] = acc[kq] + term

            @pl.when(jq == PARTS - 1)
            def _():
                core_copy(kq).start()
                core_copy(kq).wait_recv()
                total = (acc[kq, direct] + core_in[kq]).astype(jnp.bfloat16)
                stays = jnp.logical_and(home, kq == 0)

                @pl.when(stays)
                def _():
                    out[0] = total

                @pl.when(jnp.logical_not(stays))
                def _():
                    back[kq] = total
                    back_copy(kq).start()

        return carry

    lax.fori_loop(0, STEPS + LAG_SUM + LAG_DOWN, body, 0)

    def drain(s, carry):
        part_copy(s).wait_send()
        hid_copy(s).wait_send()
        return carry

    lax.fori_loop(0, STEPS, drain, 0)
    for k in range(HOPS):
        forward(k).wait_send()
        core_copy(k).wait_send()
        if k > 0:
            dispatch(k).wait_send()
            back_copy(k).wait()

    @pl.when(jnp.logical_not(home))
    def _():
        dispatch(0).wait_send()
        back_copy(0).wait()


def fused(
    incoming_activation_vectors,
    routed_specialist_pairs,
    routing_shares,
    popular_specialist_flags,
    group_quotas,
    gating_weight_stack,
    widen_weight_stack,
    contract_weight_stack,
):
    experts = popular_specialist_flags.shape[0]
    tok_rows, half_width = incoming_activation_vectors.shape
    units = gating_weight_stack.shape[1]
    width = units // PARTS
    kept_pair, target = route(routed_specialist_pairs, popular_specialist_flags, group_quotas)
    slots = experts * GROUP_QUOTA
    place = jnp.arange(slots, dtype=jnp.int32)
    place = (place // GROUP_QUOTA ^ lax.axis_index("expert")) * GROUP_QUOTA + place % GROUP_QUOTA
    hits = (place[:, None] == target[None, :]).reshape(slots, tok_rows, 2)
    select = hits.astype(jnp.bfloat16).sum(axis=2)
    packed = jnp.dot(
        select, incoming_activation_vectors, preferred_element_type=jnp.float32
    ).astype(jnp.bfloat16)
    bf16, f32 = jnp.bfloat16, jnp.float32
    dma = pltpu.SemaphoreType.DMA
    quota = GROUP_QUOTA
    summed = pl.pallas_call(
        layer_kernel,
        out_shape=jax.ShapeDtypeStruct((HOPS, quota, half_width), bf16),
        in_specs=[pl.BlockSpec(memory_space=pltpu.VMEM)] + [pl.BlockSpec(memory_space=pl.ANY)] * 3,
        out_specs=pl.BlockSpec(memory_space=pltpu.VMEM),
        scratch_shapes=[
            pltpu.VMEM((PARTS, half_width, width), bf16),
            pltpu.VMEM((PARTS, half_width, width), bf16),
            pltpu.VMEM((PARTS, width, half_width), bf16),
            pltpu.VMEM((HOPS, 2, quota, half_width), bf16),
            pltpu.VMEM((STEPS, 2, quota, width), f32),
            pltpu.VMEM((STEPS, 2, quota, width), bf16),
            pltpu.VMEM((STEPS, 2, quota, width), bf16),
            pltpu.VMEM((STEPS, 2, quota, width), bf16),
            pltpu.VMEM((HOPS, 2, quota, half_width), f32),
            pltpu.VMEM((HOPS, quota, half_width), f32),
            pltpu.VMEM((HOPS, quota, half_width), bf16),
            dma((3, PARTS)),
            dma((HOPS,)),
            dma((HOPS,)),
            dma((HOPS,)),
            dma((HOPS,)),
            dma,
            dma((STEPS,)),
            dma((STEPS,)),
            dma((STEPS,)),
            dma((STEPS,)),
            dma((HOPS,)),
            dma((HOPS,)),
            dma((HOPS,)),
            dma((HOPS,)),
        ],
        compiler_params=pltpu.CompilerParams(
            collective_id=0, has_side_effects=True, vmem_limit_bytes=60 * 1024 * 1024
        ),
        name="expert_layer",
    )(
        packed.reshape(HOPS, quota, half_width),
        gating_weight_stack,
        widen_weight_stack,
        contract_weight_stack,
    )
    weights_kept = jnp.where(kept_pair, routing_shares.reshape(-1), 0.0)
    pick = jnp.where(hits, weights_kept.reshape(1, tok_rows, 2), 0.0).sum(axis=2)
    return jnp.dot(
        pick.T,
        summed.reshape(slots, half_width).astype(jnp.float32),
        precision=lax.Precision.HIGHEST,
    ).astype(jnp.bfloat16)


def solution(mesh):
    shape = mesh.shape
    square = shape["dp"] == 2 and shape["tensor"] == 2 and shape["expert"] == EXPERTS
    local = fused if square else gathered
    placed = (
        P(("group", "expert", "dp"), "tensor"),
        P(("group", "expert", "dp"), None),
        P(("group", "expert", "dp"), None),
        P("group"),
        P("group"),
        P("dp", ("expert", "tensor")),
        P("dp", ("expert", "tensor")),
        P(("expert", "tensor"), "dp"),
    )
    return jax.shard_map(
        local,
        mesh=mesh,
        in_specs=placed,
        out_specs=P(("group", "expert", "dp"), "tensor"),
        check_vma=False,
    )
```

profile of v0, /device:TPU:0, one launch (start us, length us, event | category | flops | bytes accessed | tf_op | source)
XLA Modules:
  0.0 99.8 jit_solution(7334137914060691363)
XLA Ops:
  0.0 0.0 copy-start
  0.0 0.7 compare_select_fusion.1
  0.7 0.8 copy.23
  1.5 0.1 eq.35
  1.6 0.1 fusion.1
  1.7 0.2 reduce_window_sum.11
  1.9 0.2 select_reduce_fusion
  2.1 0.1 reduce_sum.46
  2.2 0.1 copy.25
  2.3 0.1 reduce_sum.44
  2.4 0.1 copy.24
  2.5 0.7 add_select_fusion
  3.2 0.7 broadcast_select_fusion
  3.9 0.1 fusion.2
  4.0 0.1 fusion
  4.1 0.0 copy-done
  4.1 1.0 %convolution_convert_fusion = bf16[128,1536]{1,0:T(8,128)(2,1)} fusion(bf16[128,64]{0,1:T(8,128)(2,1)S(1)} %fusion.2, bf16[64,1536]{1,0:T(8,128)(2,1)S(1)} %copy-done), kind=kOutput, calls=%fused_computation | convolution fusion | flops 25362432 | bytes 606208 | tf_op jit(solution)/shard_map/dot_general | solution.py:350
  5.1 92.7 %expert_layer.1 = bf16[4,32,1536]{2,1,0:T(8,128)(2,1)} custom-call(bf16[4,32,1536]{2,1,0:T(8,128)(2,1)} %bitcast.7, bf16[1536,4096]{1,0:T(8,128)(2,1)} %gate_hbm.1, bf16[1536,4096]{1,0:T(8,128)(2,1)} %up_hbm.1, bf16[4096,1536]{1,0:T(8,128)(2,1)} %down_hbm.1), custom_call_target="tpu_custom_call" | custom-call | tf_op jit(solution)/shard_map/expert_layer/pallas_call | solution.py:356
  97.8 2.0 %convolution_convert_fusion.1 = bf16[64,1536]{1,0:T(8,128)(2,1)} fusion(f32[128,64]{0,1:T(8,128)S(1)} %fusion, bf16[128,1536]{1,0:T(8,128)(2,1)} %bitcast.6), kind=kOutput, calls=%fused_computation.1 | convolution fusion | flops 151093248 | bytes 622592 | tf_op jit(solution)/shard_map/dot_general | solution.py:400
  (1 shorter events, 0.0 us)
Async XLA Ops:
  0.0 4.1 %copy-start = (bf16[64,1536]{1,0:T(8,128)(2,1)S(1)}, bf16[64,1536]{1,0:T(8,128)(2,1)}, u32[]{:S(2)}) copy-start(bf16[64,1536]{1,0:T(8,128)(2,1)} %param.8) | copy-start | bytes 589828
where the time goes:
time: 100 us; the launch traced here: 99.8 us
  Pallas kernels  92.7 us (93%)
  matrix products  3.03 us (3%)
  other arithmetic  2.72 us (3%)
  local copies, waits for them, and re-layouts  1.32 us (1%)
    pallas_call x1, Pallas kernels, fused(): pl.pallas_call(layer_kernel, out_shape=jax.ShapeDtypeStruct((HOPS, quota,...  92.7 us

commit v1 on v0

--- a/solution.py
+++ b/solution.py
@@ -79,21 +79,12 @@
     return mixed.astype(jnp.bfloat16)
 
 
-def route(routed_specialist_pairs, popular_specialist_flags, group_quotas):
-    experts = popular_specialist_flags.shape[0]
-    pair_ids = routed_specialist_pairs.reshape(-1)
-    onehot = (pair_ids[:, None] == jnp.arange(experts, dtype=jnp.int32)[None, :]).astype(jnp.int32)
-    slot_rank = jnp.sum((jnp.cumsum(onehot, axis=0) - onehot) * onehot, axis=1)
-    quota_bound = jnp.where(popular_specialist_flags == 1, GROUP_QUOTA, group_quotas)
-    kept_pair = slot_rank < jnp.sum(onehot * quota_bound[None, :], axis=1)
-    return kept_pair, jnp.where(kept_pair, pair_ids * GROUP_QUOTA + slot_rank, -1)
-
-
 HOPS = 4
 PARTS = 4
 STEPS = HOPS * PARTS
 LAG_SUM = 3
 LAG_DOWN = 3
+AHEAD = 2
 
 
 def flip(e, k):
@@ -103,7 +94,11 @@
 
 
 def layer_kernel(
-    packed,
+    flags,
+    quotas,
+    tokens,
+    pairs,
+    shares,
     gate_hbm,
     up_hbm,
     down_hbm,
@@ -111,6 +106,9 @@
     gate_w,
     up_w,
     down_w,
+    packed,
+    picks,
+    returned,
     rows,
     keep,
     part_out,
@@ -124,7 +122,6 @@
     disp_recv,
     fwd_send,
     fwd_recv,
-    self_sem,
     part_send,
     part_recv,
     hid_send,
@@ -170,9 +167,6 @@
             packed.at[k], rows.at[k, direct], disp_send.at[k], disp_recv.at[k], far(k)
         )
 
-    def dispatch_self():
-        return pltpu.make_async_copy(packed.at[0], rows.at[0, direct], self_sem)
-
     def forward(k):
         return remote(
             rows.at[k, direct], rows.at[k, direct], fwd_send.at[k], fwd_recv.at[k], sibling
@@ -188,41 +182,71 @@
         return remote(acc.at[k, 1 - direct], core_in.at[k], core_send.at[k], core_recv.at[k], sibling)
 
     def back_copy(k):
-        return remote(back.at[k], out.at[k], back_send.at[k], back_recv.at[k], far(k))
-
-    for j in range(PARTS):
+        return remote(back.at[k], returned.at[k], back_send.at[k], back_recv.at[k], far(k))
+
+    for j in range(AHEAD):
         weight_copy(0, j).start()
         weight_copy(1, j).start()
-    for j in range(PARTS):
-        weight_copy(2, j).start()
 
     barrier = pltpu.get_barrier_semaphore()
     for target in (sibling, across, far(1), far(2), far(3)):
         pl.semaphore_signal(barrier, inc=1, device_id=target, device_id_type=mesh_ids)
 
+    @pl.when(jnp.logical_not(home))
+    def _():
+        pl.semaphore_signal(barrier, inc=1, device_id=far(0), device_id_type=mesh_ids)
+
+    count = tokens.shape[0]
+    grid = (quota, count)
+    first = jnp.broadcast_to(pairs[0:1, :], grid)
+    second = jnp.broadcast_to(pairs[1:2, :], grid)
+    first_share = jnp.broadcast_to(shares[0:1, :], grid)
+    second_share = jnp.broadcast_to(shares[1:2, :], grid)
+    slot = lax.broadcasted_iota(jnp.int32, grid, 0)
+    square = (count, count)
+    earlier = (
+        lax.broadcasted_iota(jnp.int32, square, 0) < lax.broadcasted_iota(jnp.int32, square, 1)
+    )
+    earlier = jnp.where(earlier, 1.0, 0.0).astype(jnp.bfloat16)
+
+    def choose(k):
+        expert = flip(e, k)
+        limit = jnp.where(flags[expert] == 1, GROUP_QUOTA, quotas[expert])
+        is_first = first == expert
+        named = jnp.logical_or(is_first, second == expert)
+        ones = jnp.where(named, 1.0, 0.0)
+        rank = jnp.dot(ones.astype(jnp.bfloat16), earlier, preferred_element_type=jnp.float32)
+        rank = rank.astype(jnp.int32)
+        hit = jnp.logical_and(jnp.logical_and(named, rank == slot), slot < limit)
+        picks[k] = jnp.where(hit, jnp.where(is_first, first_share, second_share), 0.0)
+        chosen = jnp.where(hit, 1.0, 0.0).astype(jnp.bfloat16)
+        return jnp.dot(chosen, tokens[...], preferred_element_type=jnp.float32).astype(
+            jnp.bfloat16
+        )
+
+    nearest = choose(0)
+
     @pl.when(home)
     def _():
+        rows[0, direct] = nearest
         pl.semaphore_wait(barrier, 5)
-        dispatch_self().start()
 
     @pl.when(jnp.logical_not(home))
     def _():
-        pl.semaphore_signal(barrier, inc=1, device_id=far(0), device_id_type=mesh_ids)
+        packed[0] = nearest
         pl.semaphore_wait(barrier, 6)
         dispatch(0).start()
 
     for k in range(1, HOPS):
+        packed[k] = choose(k)
+
+    @pl.when(jnp.logical_not(home))
+    def _():
+        dispatch(0).wait_recv()
+
+    forward(0).start()
+    for k in range(1, HOPS):
         dispatch(k).start()
-
-    @pl.when(home)
-    def _():
-        dispatch_self().wait()
-
-    @pl.when(jnp.logical_not(home))
-    def _():
-        dispatch(0).wait_recv()
-
-    forward(0).start()
     forward(0).wait_recv()
 
     def body(s, carry):
@@ -239,6 +263,15 @@
             def _():
                 weight_copy(0, j).wait()
                 weight_copy(1, j).wait()
+
+                @pl.when(j + AHEAD < PARTS)
+                def _():
+                    weight_copy(0, j + AHEAD).start()
+                    weight_copy(1, j + AHEAD).start()
+
+            @pl.when(jnp.logical_and(s >= AHEAD, s < PARTS + AHEAD))
+            def _():
+                weight_copy(2, s - AHEAD).start()
 
             block = rows[k].reshape(2 * quota, rows.shape[3])
             gate = jnp.dot(block, gate_w[j], preferred_element_type=jnp.float32)
@@ -297,7 +330,7 @@
 
                 @pl.when(stays)
                 def _():
-                    out[0] = total
+                    returned[0] = total
 
                 @pl.when(jnp.logical_not(stays))
                 def _():
@@ -307,6 +340,27 @@
         return carry
 
     lax.fori_loop(0, STEPS + LAG_SUM + LAG_DOWN, body, 0)
+
+    def mix(k):
+        pick = picks[k]
+        term = jnp.zeros(tokens.shape, jnp.float32)
+        for _ in range(3):
+            piece = pick.astype(jnp.bfloat16)
+            term += lax.dot_general(
+                piece, returned[k], (((0,), (0,)), ((), ())), preferred_element_type=jnp.float32
+            )
+            pick = pick - piece.astype(jnp.float32)
+        return term
+
+    @pl.when(jnp.logical_not(home))
+    def _():
+        back_copy(0).wait_recv()
+
+    total = mix(0)
+    for k in range(1, HOPS):
+        back_copy(k).wait_recv()
+        total += mix(k)
+    out[...] = total.astype(out.dtype)
 
     def drain(s, carry):
         part_copy(s).wait_send()
@@ -319,12 +373,12 @@
         core_copy(k).wait_send()
         if k > 0:
             dispatch(k).wait_send()
-            back_copy(k).wait()
+            back_copy(k).wait_send()
 
     @pl.when(jnp.logical_not(home))
     def _():
         dispatch(0).wait_send()
-        back_copy(0).wait()
+        back_copy(0).wait_send()
 
 
 def fused(
@@ -337,31 +391,25 @@
     widen_weight_stack,
     contract_weight_stack,
 ):
-    experts = popular_specialist_flags.shape[0]
     tok_rows, half_width = incoming_activation_vectors.shape
-    units = gating_weight_stack.shape[1]
-    width = units // PARTS
-    kept_pair, target = route(routed_specialist_pairs, popular_specialist_flags, group_quotas)
-    slots = experts * GROUP_QUOTA
-    place = jnp.arange(slots, dtype=jnp.int32)
-    place = (place // GROUP_QUOTA ^ lax.axis_index("expert")) * GROUP_QUOTA + place % GROUP_QUOTA
-    hits = (place[:, None] == target[None, :]).reshape(slots, tok_rows, 2)
-    select = hits.astype(jnp.bfloat16).sum(axis=2)
-    packed = jnp.dot(
-        select, incoming_activation_vectors, preferred_element_type=jnp.float32
-    ).astype(jnp.bfloat16)
+    width = gating_weight_stack.shape[1] // PARTS
     bf16, f32 = jnp.bfloat16, jnp.float32
     dma = pltpu.SemaphoreType.DMA
     quota = GROUP_QUOTA
-    summed = pl.pallas_call(
+    vmem = pl.BlockSpec(memory_space=pltpu.VMEM)
+    smem = pl.BlockSpec(memory_space=pltpu.SMEM)
+    return pl.pallas_call(
         layer_kernel,
-        out_shape=jax.ShapeDtypeStruct((HOPS, quota, half_width), bf16),
-        in_specs=[pl.BlockSpec(memory_space=pltpu.VMEM)] + [pl.BlockSpec(memory_space=pl.ANY)] * 3,
-        out_specs=pl.BlockSpec(memory_space=pltpu.VMEM),
+        out_shape=jax.ShapeDtypeStruct((tok_rows, half_width), bf16),
+        in_specs=[smem] * 2 + [vmem] * 3 + [pl.BlockSpec(memory_space=pl.ANY)] * 3,
+        out_specs=vmem,
         scratch_shapes=[
             pltpu.VMEM((PARTS, half_width, width), bf16),
             pltpu.VMEM((PARTS, half_width, width), bf16),
             pltpu.VMEM((PARTS, width, half_width), bf16),
+            pltpu.VMEM((HOPS, quota, half_width), bf16),
+            pltpu.VMEM((HOPS, quota, tok_rows), f32),
+            pltpu.VMEM((HOPS, quota, half_width), bf16),
             pltpu.VMEM((HOPS, 2, quota, half_width), bf16),
             pltpu.VMEM((STEPS, 2, quota, width), f32),
             pltpu.VMEM((STEPS, 2, quota, width), bf16),
@@ -375,7 +423,6 @@
             dma((HOPS,)),
             dma((HOPS,)),
             dma((HOPS,)),
-            dma,
             dma((STEPS,)),
             dma((STEPS,)),
             dma((STEPS,)),
@@ -390,18 +437,15 @@
         ),
         name="expert_layer",
     )(
-        packed.reshape(HOPS, quota, half_width),
+        popular_specialist_flags,
+        group_quotas,
+        incoming_activation_vectors,
+        routed_specialist_pairs.T,
+        routing_shares.T,
         gating_weight_stack,
         widen_weight_stack,
         contract_weight_stack,
     )
-    weights_kept = jnp.where(kept_pair, routing_shares.reshape(-1), 0.0)
-    pick = jnp.where(hits, weights_kept.reshape(1, tok_rows, 2), 0.0).sum(axis=2)
-    return jnp.dot(
-        pick.T,
-        summed.reshape(slots, half_width).astype(jnp.float32),
-        precision=lax.Precision.HIGHEST,
-    ).astype(jnp.bfloat16)
 
 
 def solution(mesh):

time: 100 us -> 96.7 us (0.967)
  matrix products: 3.03 us -> 0 us
  other arithmetic: 2.72 us -> 0 us
  Pallas kernels: 92.7 us -> 94.9 us
    dot_general x2 -> x0, matrix products: 3.03 us -> none  [the longest x1 1.99 us: fused(): jnp.dot(pick.T, summed.reshape(slots, half_width).astype(jnp.float32), pr...]
    pallas_call x1, Pallas kernels: 92.7 us -> 94.9 us  [fused(): pl.pallas_call(layer_kernel, out_shape=jax.ShapeDtypeStruct((tok_rows, ha...]
    select_n x3 -> x0, other arithmetic: 2.1 us -> none  [the longest x1 0.71 us: route(): jnp.where(popular_specialist_flags == 1, GROUP_QUOTA, group_quotas)]
where the time goes in v1:
time: 96.7 us; the launch traced here: 96.5 us
  Pallas kernels  94.9 us (98%)
  local copies, waits for them, and re-layouts  1.62 us (2%)
    pallas_call x1, Pallas kernels, fused(): pl.pallas_call(layer_kernel, out_shape=jax.ShapeDtypeStruct((tok_rows, ha...  94.9 us

profile of v1, /device:TPU:0, one launch (start us, length us, event | category | flops | bytes accessed | tf_op | source)
XLA Modules:
  0.0 96.5 jit_solution(160233241498959085)
XLA Ops:
  0.0 94.9 %expert_layer.1 = bf16[64,1536]{1,0:T(8,128)(2,1)} custom-call(s32[4]{0:T(128)} %flags.1, s32[4]{0:T(128)} %quotas.1, bf16[64,1536]{1,0:T(8,128)(2,1)} %tokens.1, s32[2,64]{1,0:T(2,128)} %bitcast.2, f32[2,64]{1,0:T(2,128)} %bitcast.3, bf16[1536,4096]{1,0:T(8,128)(2,1)} %gate_hbm.1, bf16[1536,4096]{1,0:T(8,128)(2,1)} %up_hbm.1, bf16[4096,1536]{1,0:T(8,128)(2,1)} %down_hbm.1), custom_call_target="tpu_custom_call" | custom-call | tf_op jit(solution)/shard_map/expert_layer/pallas_call | solution.py:401
  94.9 1.6 %copy.10 = bf16[64,1536]{1,0:T(8,128)(2,1)} copy(bf16[64,1536]{1,0:T(8,128)(2,1)} %expert_layer.1) | data formatting | bytes 393216

commit v2 on v1

--- a/solution.py
+++ b/solution.py
@@ -88,8 +88,8 @@
 
 
 def flip(e, k):
-    low = lax.rem(lax.rem(e, 2) + lax.rem(k, 2), 2)
-    high = lax.rem(lax.div(e, 2) + lax.div(k, 2), 2)
+    low = lax.rem(lax.rem(e, 2) + lax.div(k, 2), 2)
+    high = lax.rem(lax.div(e, 2) + lax.div(k, 2) + lax.rem(k, 2), 2)
     return low + 2 * high
 
 
@@ -172,8 +172,10 @@
             rows.at[k, direct], rows.at[k, direct], fwd_send.at[k], fwd_recv.at[k], sibling
         )
 
-    def part_copy(s):
-        return remote(part_out.at[s], part_in.at[s], part_send.at[s], part_recv.at[s], across)
+    def part_copy(s, i):
+        return remote(
+            part_out.at[s, i], part_in.at[s, i], part_send.at[s, i], part_recv.at[s, i], across
+        )
 
     def hid_copy(s):
         return remote(hid.at[s, 0], hid.at[s, 1], hid_send.at[s], hid_recv.at[s], across)
@@ -277,10 +279,11 @@
             gate = jnp.dot(block, gate_w[j], preferred_element_type=jnp.float32)
             keep[s, 0] = gate[:quota]
             part_out[s, 0] = gate[quota:].astype(jnp.bfloat16)
+            part_copy(s, 0).start()
             up = jnp.dot(block, up_w[j], preferred_element_type=jnp.float32)
             keep[s, 1] = up[:quota]
             part_out[s, 1] = up[quota:].astype(jnp.bfloat16)
-            part_copy(s).start()
+            part_copy(s, 1).start()
 
             @pl.when(jnp.logical_and(j == PARTS // 2, k < HOPS - 1))
             def _():
@@ -291,7 +294,8 @@
 
         @pl.when(jnp.logical_and(h >= 0, h < STEPS))
         def _():
-            part_copy(h).wait_recv()
+            part_copy(h, 0).wait_recv()
+            part_copy(h, 1).wait_recv()
             gate = keep[h, 0] + part_in[h, 0].astype(jnp.float32)
             up = keep[h, 1] + part_in[h, 1].astype(jnp.float32)
             hid[h, 0] = (gate / (1.0 + jnp.exp(-gate)) * up).astype(jnp.bfloat16)
@@ -363,7 +367,8 @@
     out[...] = total.astype(out.dtype)
 
     def drain(s, carry):
-        part_copy(s).wait_send()
+        part_copy(s, 0).wait_send()
+        part_copy(s, 1).wait_send()
         hid_copy(s).wait_send()
         return carry
 
@@ -423,8 +428,8 @@
             dma((HOPS,)),
             dma((HOPS,)),
             dma((HOPS,)),
-            dma((STEPS,)),
-            dma((STEPS,)),
+            dma((STEPS, 2)),
+            dma((STEPS, 2)),
             dma((STEPS,)),
             dma((STEPS,)),
             dma((HOPS,)),

time: 96.7 us -> 95 us (0.982)
  Pallas kernels: 94.9 us -> 93.2 us
    pallas_call x1, Pallas kernels: 94.9 us -> 93.2 us  [fused(): pl.pallas_call(layer_kernel, out_shape=jax.ShapeDtypeStruct((tok_rows, ha...]
where the time goes in v2:
time: 95 us; the launch traced here: 94.8 us
  Pallas kernels  93.2 us (98%)
  local copies, waits for them, and re-layouts  1.62 us (2%)
    pallas_call x1, Pallas kernels, fused(): pl.pallas_call(layer_kernel, out_shape=jax.ShapeDtypeStruct((tok_rows, ha...  93.2 us

profile of v2, /device:TPU:0, one launch (start us, length us, event | category | flops | bytes accessed | tf_op | source)
XLA Modules:
  0.0 94.8 jit_solution(10204480386249788078)
XLA Ops:
  0.0 93.2 %expert_layer.1 = bf16[64,1536]{1,0:T(8,128)(2,1)} custom-call(s32[4]{0:T(128)} %flags.1, s32[4]{0:T(128)} %quotas.1, bf16[64,1536]{1,0:T(8,128)(2,1)} %tokens.1, s32[2,64]{1,0:T(2,128)} %bitcast.2, f32[2,64]{1,0:T(2,128)} %bitcast.3, bf16[1536,4096]{1,0:T(8,128)(2,1)} %gate_hbm.1, bf16[1536,4096]{1,0:T(8,128)(2,1)} %up_hbm.1, bf16[4096,1536]{1,0:T(8,128)(2,1)} %down_hbm.1), custom_call_target="tpu_custom_call" | custom-call | tf_op jit(solution)/shard_map/expert_layer/pallas_call | solution.py:406
  93.2 1.6 %copy.10 = bf16[64,1536]{1,0:T(8,128)(2,1)} copy(bf16[64,1536]{1,0:T(8,128)(2,1)} %expert_layer.1) | data formatting | bytes 393216

commit v3 on v2

--- a/solution.py
+++ b/solution.py
@@ -106,6 +106,9 @@
     gate_w,
     up_w,
     down_w,
+    own_pairs,
+    src_pairs,
+    src_tokens,
     packed,
     picks,
     returned,
@@ -118,6 +121,8 @@
     core_in,
     back,
     w_sem,
+    swap_send,
+    swap_recv,
     disp_send,
     disp_recv,
     fwd_send,
@@ -149,6 +154,9 @@
     def far(k):
         return {"expert": flip(e, k), "dp": t, "tensor": d}
 
+    def along(k):
+        return {"expert": flip(e, k), "dp": d, "tensor": t}
+
     sibling = {"expert": e, "dp": d, "tensor": 1 - t}
     across = {"expert": e, "dp": 1 - d, "tensor": t}
 
@@ -162,9 +170,13 @@
             device_id_type=mesh_ids,
         )
 
+    def swap(i):
+        src, dst = ((own_pairs, src_pairs), (tokens, src_tokens))[i]
+        return remote(src, dst, swap_send.at[i], swap_recv.at[i], far(0))
+
     def dispatch(k):
         return remote(
-            packed.at[k], rows.at[k, direct], disp_send.at[k], disp_recv.at[k], far(k)
+            packed.at[k], rows.at[k, direct], disp_send.at[k], disp_recv.at[k], along(k)
         )
 
     def forward(k):
@@ -196,14 +208,11 @@
 
     @pl.when(jnp.logical_not(home))
     def _():
-        pl.semaphore_signal(barrier, inc=1, device_id=far(0), device_id_type=mesh_ids)
+        for target in (far(0), along(1), along(2), along(3)):
+            pl.semaphore_signal(barrier, inc=1, device_id=target, device_id_type=mesh_ids)
 
     count = tokens.shape[0]
     grid = (quota, count)
-    first = jnp.broadcast_to(pairs[0:1, :], grid)
-    second = jnp.broadcast_to(pairs[1:2, :], grid)
-    first_share = jnp.broadcast_to(shares[0:1, :], grid)
-    second_share = jnp.broadcast_to(shares[1:2, :], grid)
     slot = lax.broadcasted_iota(jnp.int32, grid, 0)
     square = (count, count)
     earlier = (
@@ -211,43 +220,54 @@
     )
     earlier = jnp.where(earlier, 1.0, 0.0).astype(jnp.bfloat16)
 
-    def choose(k):
+    own_pairs[...] = jnp.zeros(own_pairs.shape, jnp.int32)
+    own_pairs[0:2, 0:count] = pairs[...]
+
+    @pl.when(home)
+    def _():
+        src_pairs[...] = own_pairs[...]
+        src_tokens[...] = tokens[...]
+        pl.semaphore_wait(barrier, 5)
+
+    @pl.when(jnp.logical_not(home))
+    def _():
+        pl.semaphore_wait(barrier, 9)
+        swap(0).start()
+        swap(1).start()
+
+    def slots_of(k, named_by):
         expert = flip(e, k)
         limit = jnp.where(flags[expert] == 1, GROUP_QUOTA, quotas[expert])
-        is_first = first == expert
-        named = jnp.logical_or(is_first, second == expert)
+        is_first = jnp.broadcast_to(named_by[0:1, 0:count], grid) == expert
+        is_second = jnp.broadcast_to(named_by[1:2, 0:count], grid) == expert
+        named = jnp.logical_or(is_first, is_second)
         ones = jnp.where(named, 1.0, 0.0)
         rank = jnp.dot(ones.astype(jnp.bfloat16), earlier, preferred_element_type=jnp.float32)
         rank = rank.astype(jnp.int32)
-        hit = jnp.logical_and(jnp.logical_and(named, rank == slot), slot < limit)
-        picks[k] = jnp.where(hit, jnp.where(is_first, first_share, second_share), 0.0)
+        return jnp.logical_and(jnp.logical_and(named, rank == slot), slot < limit), is_first
+
+    def choose(k):
+        hit, _ = slots_of(k, src_pairs)
         chosen = jnp.where(hit, 1.0, 0.0).astype(jnp.bfloat16)
-        return jnp.dot(chosen, tokens[...], preferred_element_type=jnp.float32).astype(
+        return jnp.dot(chosen, src_tokens[...], preferred_element_type=jnp.float32).astype(
             jnp.bfloat16
         )
 
-    nearest = choose(0)
-
-    @pl.when(home)
-    def _():
-        rows[0, direct] = nearest
-        pl.semaphore_wait(barrier, 5)
+    first_share = jnp.broadcast_to(shares[0:1, :], grid)
+    second_share = jnp.broadcast_to(shares[1:2, :], grid)
+    for k in range(HOPS):
+        hit, is_first = slots_of(k, own_pairs)
+        picks[k] = jnp.where(hit, jnp.where(is_first, first_share, second_share), 0.0)
 
     @pl.when(jnp.logical_not(home))
     def _():
-        packed[0] = nearest
-        pl.semaphore_wait(barrier, 6)
-        dispatch(0).start()
-
+        swap(0).wait_recv()
+        swap(1).wait_recv()
+
+    rows[0, direct] = choose(0)
+    forward(0).start()
     for k in range(1, HOPS):
         packed[k] = choose(k)
-
-    @pl.when(jnp.logical_not(home))
-    def _():
-        dispatch(0).wait_recv()
-
-    forward(0).start()
-    for k in range(1, HOPS):
         dispatch(k).start()
     forward(0).wait_recv()
 
@@ -382,7 +402,8 @@
 
     @pl.when(jnp.logical_not(home))
     def _():
-        dispatch(0).wait_send()
+        swap(0).wait_send()
+        swap(1).wait_send()
         back_copy(0).wait_send()
 
 
@@ -412,6 +433,9 @@
             pltpu.VMEM((PARTS, half_width, width), bf16),
             pltpu.VMEM((PARTS, half_width, width), bf16),
             pltpu.VMEM((PARTS, width, half_width), bf16),
+            pltpu.VMEM((8, 128), jnp.int32),
+            pltpu.VMEM((8, 128), jnp.int32),
+            pltpu.VMEM((tok_rows, half_width), bf16),
             pltpu.VMEM((HOPS, quota, half_width), bf16),
             pltpu.VMEM((HOPS, quota, tok_rows), f32),
             pltpu.VMEM((HOPS, quota, half_width), bf16),
@@ -424,6 +448,8 @@
             pltpu.VMEM((HOPS, quota, half_width), f32),
             pltpu.VMEM((HOPS, quota, half_width), bf16),
             dma((3, PARTS)),
+            dma((2,)),
+            dma((2,)),
             dma((HOPS,)),
             dma((HOPS,)),
             dma((HOPS,)),

time: 95 us -> 94.9 us (level)
  no operation moved by 1% of the time
where the time goes in v3:
time: 94.9 us; the launch traced here: 94.1 us
  Pallas kernels  92.5 us (97%)
  local copies, waits for them, and re-layouts  1.62 us (2%)
    pallas_call x1, Pallas kernels, fused(): pl.pallas_call(layer_kernel, out_shape=jax.ShapeDtypeStruct((tok_rows, ha...  92.5 us

profile of v3, /device:TPU:0, one launch (start us, length us, event | category | flops | bytes accessed | tf_op | source)
XLA Modules:
  0.0 94.1 jit_solution(9141372819439250870)
XLA Ops:
  0.0 92.5 %expert_layer.1 = bf16[64,1536]{1,0:T(8,128)(2,1)} custom-call(s32[4]{0:T(128)} %flags.1, s32[4]{0:T(128)} %quotas.1, bf16[64,1536]{1,0:T(8,128)(2,1)} %tokens.1, s32[2,64]{1,0:T(2,128)} %bitcast.2, f32[2,64]{1,0:T(2,128)} %bitcast.3, bf16[1536,4096]{1,0:T(8,128)(2,1)} %gate_hbm.1, bf16[1536,4096]{1,0:T(8,128)(2,1)} %up_hbm.1, bf16[4096,1536]{1,0:T(8,128)(2,1)} %down_hbm.1), custom_call_target="tpu_custom_call" | custom-call | tf_op jit(solution)/shard_map/expert_layer/pallas_call | solution.py:427
  92.5 1.6 %copy.10 = bf16[64,1536]{1,0:T(8,128)(2,1)} copy(bf16[64,1536]{1,0:T(8,128)(2,1)} %expert_layer.1) | data formatting | bytes 393216
